TPU v7x, 512 devices: a whole 4x4x16 slice. The times are simulated.
512 devices in a mesh: seq: 16 (over z_lo, y), dp: 32 (over x, z_hi, core).
Axes of the slice: x: 4, y: 4, z: 16 (z_hi: 4, z_lo: 4; z = z_hi * 4 + z_lo), core: 2. Of those that a mesh axis runs over, the one named last changes fastest.
Arguments:
- frames: bfloat16 [32, 3072, 1536], P('dp', 'seq'), may hold values from -6 to 6
- queries: bfloat16 [32, 3072, 1536], P('dp', 'seq'), may hold values from -16 to 16
- keys: bfloat16 [32, 3072, 1536], P('dp', 'seq'), may hold values from -16 to 16
- values: bfloat16 [32, 3072, 1536], P('dp', 'seq'), may hold values from -24 to 24
- lengths: int32 [32], P('dp'), may hold values from 1536 to 3072, as said below
- out_proj: bfloat16 [1536, 1536], P(None, 'dp'), may hold values from -0.15625 to 0.15625
- conv_kernel: float32 [31, 1536], replicated, may hold values from -1 to 1
- cotangent: bfloat16 [32, 3072, 1536], P('dp', 'seq'), may hold values from -6 to 6
Outputs:
- block_out: bfloat16 [32, 3072, 1536], P('dp', 'seq')
- grad_hidden: bfloat16 [32, 3072, 1536], P('dp', 'seq')
- grad_context: bfloat16 [32, 3072, 1536], P('dp', 'seq')
- grad_kernel: float32 [31, 1536], replicated
Inputs may be any that keep to these rules, and one draw needn't show every extreme that they name: `lengths`: one utterance has 3072 valid frames and another 3072 // 2.
All inputs are finite; a program needn't handle non-finite values.
Results may differ from a plain program's by a relative error of at most 0.0062.
Values may be sent and summed in bfloat16 or wider, within the bound.
No kernel may reach another device: no remote copies, remote signals or barrier semaphores. Data moves between devices by JAX's collectives and lax.ppermute only.
A program may use at most 64 MiB of HBM per device.

v0:
```python
import math
import jax
import jax.numpy as jnp
from jax import lax
from jax.sharding import PartitionSpec as P

KERNEL = 31
HEAD_DIM = 96


def with_halo(block, sides, width):
    for axis, dim in sides:
        count = lax.axis_size(axis)
        forward = [(i, i + 1) for i in range(count - 1)]
        backward = [(target, source) for source, target in forward]
        low = lax.ppermute(
            lax.slice_in_dim(block, block.shape[dim] - width, None, axis=dim), axis, forward
        )
        high = lax.ppermute(lax.slice_in_dim(block, 0, width, axis=dim), axis, backward)
        block = jnp.concatenate([low, block, high], axis=dim)
    return block


def attend_heads(query_heads, key_heads, value_heads, key_valid):
    total_frames = query_heads.shape[0]
    head_count = query_heads.shape[1]
    block_rows = math.gcd(total_frames, 1024)
    blocks = query_heads.reshape(total_frames // block_rows, block_rows, head_count, HEAD_DIM)
    softmax_scale = HEAD_DIM ** (-0.5)

    def one_block(query_block):
        scores = (
            jnp.einsum("qhe,khe->hqk", query_block, key_heads, preferred_element_type=jnp.float32)
            * softmax_scale
        )
        scores = jnp.where(key_valid[None, None, :], scores, -jnp.inf)
        largest = jnp.max(scores, axis=-1, keepdims=True)
        expd = jnp.exp(scores - largest)
        weights = (expd / jnp.sum(expd, axis=-1, keepdims=True)).astype(jnp.bfloat16)
        return jnp.einsum(
            "hqk,khe->qhe", weights, value_heads, preferred_element_type=jnp.float32
        ).astype(jnp.bfloat16)

    return lax.map(one_block, blocks).reshape(total_frames, head_count * HEAD_DIM)


def local(frames, queries, keys, values, lengths, out_proj, conv_kernel, cotangent):
    frames_dev = frames.shape[1]
    groups = lax.axis_size("seq")
    length_all = frames_dev * groups
    half_width = KERNEL // 2
    first_frame = lax.axis_index("seq") * frames_dev
    valid_local = first_frame + jnp.arange(frames_dev, dtype=jnp.int32) < lengths[0]
    key_valid = jnp.arange(length_all, dtype=jnp.int32) < lengths[0]
    query_group, key_group, value_group = (
        lax.all_to_all(queries, "seq", split_axis=2, concat_axis=1, tiled=True),
        lax.all_to_all(keys, "seq", split_axis=2, concat_axis=1, tiled=True),
        lax.all_to_all(values, "seq", split_axis=2, concat_axis=1, tiled=True),
    )
    head_count = query_group.shape[2] // HEAD_DIM
    context_heads = attend_heads(
        query_group[0].reshape(length_all, head_count, HEAD_DIM),
        key_group[0].reshape(length_all, head_count, HEAD_DIM),
        value_group[0].reshape(length_all, head_count, HEAD_DIM),
        key_valid,
    )
    context = lax.all_to_all(context_heads[None], "seq", split_axis=1, concat_axis=2, tiled=True)[0]
    mixed = jnp.dot(
        context,
        lax.all_gather(out_proj, "dp", axis=1, tiled=True),
        preferred_element_type=jnp.float32,
    )
    hidden = (frames[0].astype(jnp.float32) + mixed).astype(jnp.bfloat16)
    conv_input = jnp.where(valid_local[:, None], hidden, jnp.zeros((), jnp.bfloat16))
    padded = with_halo(conv_input[None], (("seq", 1),), half_width)[0]
    conv = jnp.zeros((frames_dev, conv_input.shape[1]), jnp.float32)
    for offset in range(KERNEL):
        conv = conv + conv_kernel[offset] * padded[offset : offset + frames_dev].astype(jnp.float32)
    sigma = jax.nn.sigmoid(conv)
    block_out = (hidden.astype(jnp.float32) + conv * sigma).astype(jnp.bfloat16)
    grad_out = cotangent[0].astype(jnp.float32)
    conv_grad = (grad_out * sigma * (1.0 + conv * (1.0 - sigma))).astype(jnp.bfloat16)
    grad_float = conv_grad.astype(jnp.float32)
    kernel_terms = []
    for offset in range(KERNEL):
        kernel_terms.append(
            jnp.sum(grad_float * padded[offset : offset + frames_dev].astype(jnp.float32), axis=0)
        )
    total_count = length_all * lax.axis_size("dp")
    grad_kernel = lax.psum(jnp.stack(kernel_terms), ("seq", "dp")) / math.sqrt(total_count)
    grad_padded = with_halo(conv_grad[None], (("seq", 1),), half_width)[0]
    back = jnp.zeros((frames_dev, conv_input.shape[1]), jnp.float32)
    for offset in range(KERNEL):
        begin = 2 * half_width - offset
        back = back + conv_kernel[offset] * grad_padded[begin : begin + frames_dev].astype(
            jnp.float32
        )
    grad_hidden = (grad_out + jnp.where(valid_local[:, None], back, 0.0)).astype(jnp.bfloat16)
    grad_context = lax.dot_general(
        grad_hidden,
        lax.all_gather(out_proj, "dp", axis=1, tiled=True),
        (((1,), (1,)), ((), ())),
        preferred_element_type=jnp.float32,
    )
    grad_context = grad_context.astype(jnp.bfloat16)
    return (block_out[None], grad_hidden[None], grad_context[None], grad_kernel)


def solution(mesh):
    in_specs = (
        P("dp", "seq", None),
        P("dp", "seq", None),
        P("dp", "seq", None),
        P("dp", "seq", None),
        P("dp"),
        P(None, "dp"),
        P(),
        P("dp", "seq", None),
    )
    out_specs = (P("dp", "seq", None), P("dp", "seq", None), P("dp", "seq", None), P())
    return jax.shard_map(local, mesh=mesh, in_specs=in_specs, out_specs=out_specs, check_vma=False)
```

profile of v0, /device:TPU:1, one launch (start us, length us, event | category | flops | bytes accessed | tf_op | source)
XLA Modules:
  0.0 701.6 jit_solution(153183562824020149)
XLA Ops:
  7.2 3.5 copy.31
  11.2 8.8 %reduce.66 = bf16[1536,192]{1,0:T(8,128)(2,1)S(1)} reduce(bf16[1536,1,192]{2,1,0:T(2,128)(2,1)S(1)} %bitcast.821, bf16[]{:T(256)} %broadcast.335), dimensions={1}, to_apply=%bitcast.766.reduce_sub_computation | reduce | bytes 1179650
  20.0 1.7 reshape.719
  21.8 9.2 %all-to-all-start = ((bf16[16,2,9216]{2,1,0:T(2,128)(2,1)}), bf16[16,2,9216]{2,1,0:T(2,128)(2,1)S(1)}, u32[]{:S(2)}, u32[]{:S(2)}) async-start(bf16[16,2,9216]{2,1,0:T(2,128)(2,1)} %reshape.719), calls=%async_computation | async-start | bytes 1179648 | tf_op jit(solution)/shard_map/all_to_all | solution.py:56
  32.2 8.8 %reduce.67 = bf16[1536,192]{1,0:T(8,128)(2,1)S(1)} reduce(bf16[1536,1,192]{2,1,0:T(2,128)(2,1)S(1)} %bitcast.823, bf16[]{:T(256)} %broadcast.335), dimensions={1}, to_apply=%bitcast.768.reduce_sub_computation | reduce | bytes 1179650
  41.0 1.7 reshape.721
  42.7 2.8 all-to-all-done
  45.5 5.7 all-to-all-start.1
  52.5 8.8 %reduce.68 = bf16[1536,192]{1,0:T(8,128)(2,1)S(1)} reduce(bf16[1536,1,192]{2,1,0:T(2,128)(2,1)S(1)} %bitcast.824, bf16[]{:T(256)} %broadcast.335), dimensions={1}, to_apply=%bitcast.770.reduce_sub_computation | reduce | bytes 1179650
  61.3 1.7 reshape.723
  63.0 2.2 all-to-all-done.1
  65.2 6.1 all-to-all-start.2
  78.0 1.3 copy.36
  80.2 5.1 all-to-all-done.2
  85.3 4.8 reshape.724
  91.8 1.3 copy.39
  94.0 28.7 %while.11 = (s32[]{:T(128)}, bf16[3,1024,1,96]{1,3,2,0:T(8,128)(2,1)S(1)}, bf16[3,1024,1,96]{1,3,2,0:T(8,128)(2,1)S(1)}, bf16[3072,1,96]{0,2,1:T(8,128)(2,1)S(1)...) while((s32[]{:T(128)}, bf16[3,1024,1,96]{1,3,2,0:T(8,128)(2,1)S(1)}, ...), condition=%wide.region_3.4_spmd.clone, body=%wide.region_0.3_spmd.clone.sunk | while | flops 1245807616 | bytes 39354456 | solution.py:44
  94.8 2.1 fusion.344
  96.9 2.7 fusion.345
  99.6 4.0 fusion.346
  104.3 2.1 fusion.344
  106.4 2.7 fusion.345
  109.1 4.0 fusion.346
  113.8 2.1 fusion.344
  115.9 2.7 fusion.345
  118.6 4.0 fusion.346
  123.4 17.3 %reduce.69 = bf16[3072,96]{1,0:T(8,128)(2,1)S(1)} reduce(bf16[3072,1,96]{2,1,0:T(2,128)(2,1)S(1)} %bitcast.822, bf16[]{:T(256)} %broadcast.335), dimensions={1}, to_apply=%bitcast.772.reduce_sub_computation | reduce | bytes 1179650
  140.8 2.0 reshape.725
  142.8 6.0 all-to-all-start.3
  149.9 35.1 %all-to-all-done.3 = bf16[16,2,9216]{2,1,0:T(2,128)(2,1)S(1)} async-done(((bf16[16,2,9216]{2,1,0:T(2,128)(2,1)}), bf16[16,2,9216]{2,1,0:T(2,128)(2,1)S(1)}, u32[]{:S(2)}, u32[]{:S(2)}) %all-to-all-start.3) | async-done | bytes 589856 | tf_op jit(solution)/shard_map/all_to_all | solution.py:67
  186.1 1.6 copy.43
  188.6 1.2 copy.44
  190.8 4.0 fusion.16
  194.9 2.1 collective-permute-start
  197.1 1.3 collective-permute-start.1
  198.6 3.9 collective-permute-done.1
  202.5 6.0 fusion.208
  208.5 1.3 collective-permute-start.2
  209.8 4.0 collective-permute-start.3
  213.8 7.3 %fusion.239 = (f32[1536]{0:T(1024)S(1)}, f32[1536]{0:T(1024)S(1)}, f32[1536]{0:T(1024)S(1)}, f32[1536]{0:T(1024)S(1)}, f32[1536]{0:T(1024)S(1)}, /*index=5*/f32[...) fusion(bf16[1,15,1536]{2,1,0:T(8,128)(2,1)S(1)} %collective-permute-done.1, ...), kind=kLoop, calls=%fused_computation.457 | loop fusion | flops 67820544 | bytes 3858624 | tf_op jit(solution)/shard_map/reduce_sum | solution.py:87
  221.1 1.4 fusion.240
  224.8 1.3 fusion.238
  226.2 1.4 fusion.225
  227.9 2.8 stack.127
  230.7 6.5 fusion.209
  237.2 8.9 %fusion.17 = bf16[1,192,1536]{2,1,0:T(8,128)(2,1)} fusion(bf16[1536,1536]{0,1:T(8,128)(2,1)} %all-gather.2.cloned.1.call-done, bf16[1,192,1536]{2,1,0:T(8,128)(2,1)S(1)} %copy-done, bf16[1,192,1536]{2,1,0:T(8,128)(2,1)S(1)} %fusion.208, bf16[1,15,1536]{2,1,0:T(8,128)(2,1)S(1)} %collective-permute-done.3, ...), kind=kOutput, calls=%fused_computation.109 | convolution fusion | flops 961118208 | bytes 6770880 | tf_op jit(solution)/shard_map/dot_general | solution.py:99
  246.2 446.7 %all-reduce.2.cloned.1.call-done = f32[31,1536]{1,0:T(8,128)} async-done(((f32[31,1536]{1,0:T(8,128)}), f32[31,1536]{1,0:T(8,128)}) %all-reduce.2.cloned.1.call-update) | async-done | bytes 190480 | tf_op jit(solution)/shard_map/psum | solution.py:90
  692.9 1.6 broadcast_multiply_fusion
  (83 shorter events, 21.6 us)
Async XLA Ops:
  20.0 10.9 %copy-start.1 = (bf16[1,192,1536]{2,1,0:T(8,128)(2,1)S(1)}, bf16[1,192,1536]{2,1,0:T(8,128)(2,1)}, u32[]{:S(2)}) copy-start(bf16[1,192,1536]{2,1,0:T(8,128)(2,1)} %param.12) | copy-start | bytes 1769476
  21.8 23.8 %all-to-all-start = ((bf16[16,2,9216]{2,1,0:T(2,128)(2,1)}), bf16[16,2,9216]{2,1,0:T(2,128)(2,1)S(1)}, u32[]{:S(2)}, u32[]{:S(2)}) async-start(bf16[16,2,9216]{2,1,0:T(2,128)(2,1)} %reshape.719), calls=%async_computation | async-start | bytes 1179648 | tf_op jit(solution)/shard_map/all_to_all | solution.py:56
  42.7 8.5 %copy-start.2 = (bf16[1,192,1536]{2,1,0:T(8,128)(2,1)S(1)}, bf16[1,192,1536]{2,1,0:T(8,128)(2,1)}, u32[]{:S(2)}) copy-start(bf16[1,192,1536]{2,1,0:T(8,128)(2,1)} %param.13) | copy-start | bytes 1769476
  45.5 19.7 %all-to-all-start.1 = ((bf16[16,2,9216]{2,1,0:T(2,128)(2,1)}), bf16[16,2,9216]{2,1,0:T(2,128)(2,1)S(1)}, u32[]{:S(2)}, u32[]{:S(2)}) async-start(bf16[16,2,9216]{2,1,0:T(2,128)(2,1)} %reshape.721), calls=%async_computation.1 | async-start | bytes 1179648 | tf_op jit(solution)/shard_map/all_to_all | solution.py:57
  65.2 20.1 %all-to-all-start.2 = ((bf16[16,2,9216]{2,1,0:T(2,128)(2,1)}), bf16[16,2,9216]{2,1,0:T(2,128)(2,1)}, u32[]{:S(2)}, u32[]{:S(2)}) async-start(bf16[16,2,9216]{2,1,0:T(2,128)(2,1)} %reshape.723), calls=%async_computation.2 | async-start | bytes 1179648 | tf_op jit(solution)/shard_map/all_to_all | solution.py:58
  71.4 119.4 %all-gather.2.cloned.1.call-start = ((), (), s32[]{:S(2)}) async-start(), calls=%async_computation.4 | async-start | bytes 4866048 | tf_op jit(solution)/shard_map/all_gather | solution.py:70
  91.8 2.2 copy-start.3
  140.8 8.8 %copy-start.4 = (f32[31,1536]{1,0:T(8,128)S(1)}, f32[31,1536]{1,0:T(8,128)}, u32[]{:S(2)}) copy-start(f32[31,1536]{1,0:T(8,128)} %param.16) | copy-start | bytes 571396
  142.8 42.2 %all-to-all-start.3 = ((bf16[16,2,9216]{2,1,0:T(2,128)(2,1)}), bf16[16,2,9216]{2,1,0:T(2,128)(2,1)S(1)}, u32[]{:S(2)}, u32[]{:S(2)}) async-start(bf16[16,2,9216]{2,1,0:T(2,128)(2,1)} %reshape.725), calls=%async_computation.3 | async-start | bytes 1179648 | tf_op jit(solution)/shard_map/all_to_all | solution.py:67
  148.8 544.1 %all-reduce.2.cloned.1.call-start = ((), (), s32[]{:S(2)}) async-start(), calls=%async_computation.5 | async-start | bytes 393216 | tf_op jit(solution)/shard_map/psum | solution.py:90
  188.6 2.2 copy-start.5
  194.8 7.7 %copy-start = (bf16[1,192,1536]{2,1,0:T(8,128)(2,1)S(1)}, bf16[1,192,1536]{2,1,0:T(8,128)(2,1)}, u32[]{:S(2)}) copy-start(bf16[1,192,1536]{2,1,0:T(8,128)(2,1)} %param.17) | copy-start | bytes 1769476
  194.9 3.6 collective-permute-start
  197.1 5.4 collective-permute-start.1
  208.5 22.2 %collective-permute-start.2 = (bf16[1,15,1536]{2,1,0:T(8,128)(2,1)S(1)}, bf16[1,15,1536]{2,1,0:T(8,128)(2,1)S(1)}, u32[]{:S(2)}, u32[]{:S(2)}) collective-permute-start(bf16[1,15,1536]{2,1,0:T(8,128)(2,1)S(1)} %get-tuple-element.152), channel_id=1, source_target_pairs={{32,0},{64,32},{96,64},{128,96},{160,128},{192,160},{224,192},{256... | collective-permute-start | bytes 138248 | tf_op jit(solution)/shard_map/ppermute | solution.py:19
  209.8 20.9 %collective-permute-start.3 = (bf16[1,15,1536]{2,1,0:T(8,128)(2,1)S(1)}, bf16[1,15,1536]{2,1,0:T(8,128)(2,1)S(1)}, u32[]{:S(2)}, u32[]{:S(2)}) collective-permute-start(bf16[1,15,1536]{2,1,0:T(8,128)(2,1)S(1)} %get-tuple-element.153), channel_id=1, source_target_pairs={{0,32},{32,64},{64,96},{96,128},{128,160},{160,192},{192,224},{224... | collective-permute-start | bytes 138248 | tf_op jit(solution)/shard_map/ppermute | solution.py:16
Sparse Core Ops, SparseCore 0:
  75.3 107.3 all-gather.1
  230.8 462.0 all-reduce.1
where the time goes:
time: 711 us; the launch traced here: 702 us
  waiting for transfers between devices  496 us (70%)
  other arithmetic  81.8 us (12%)
  local copies, waits for them, and re-layouts  40.2 us (6%)
  starting transfers between devices  36 us (5%)
  matrix products  31.2 us (4%)
  between operations  15.7 us (2%)
    psum x1, waiting for transfers between devices, local(): lax.psum(jnp.stack(kernel_terms), ('seq', 'dp')) / math.sqrt(total_count)  447 us
    unnamed x4, other arithmetic  43.9 us
    all_to_all x1, waiting for transfers between devices, local(): lax.all_to_all(context_heads[None], 'seq', split_axis=1, concat_axis=2, t...  35.1 us
    unnamed x25, local copies, waits for them, and re-layouts  22.1 us
  transfers between devices with their start and end apart: 10, of which 6 were waited for; matrix products, arithmetic and copies ran while one was open for 18% of the time, Pallas kernels for 0%

commit v1 on v0

--- a/solution.py
+++ b/solution.py
@@ -6,6 +6,12 @@
 
 KERNEL = 31
 HEAD_DIM = 96
+
+
+def part_page(xin, dev_axis, device_axis):
+    for dev_i in (dev_axis, device_axis):
+        xin = lax.psum(xin, dev_i)
+    return xin
 
 
 def with_halo(block, sides, width):
@@ -87,7 +93,9 @@
             jnp.sum(grad_float * padded[offset : offset + frames_dev].astype(jnp.float32), axis=0)
         )
     total_count = length_all * lax.axis_size("dp")
-    grad_kernel = lax.psum(jnp.stack(kernel_terms), ("seq", "dp")) / math.sqrt(total_count)
+    grad_kernel = part_page(jnp.stack(kernel_terms), dev_axis="seq", device_axis="dp") / math.sqrt(
+        total_count
+    )
     grad_padded = with_halo(conv_grad[None], (("seq", 1),), half_width)[0]
     back = jnp.zeros((frames_dev, conv_input.shape[1]), jnp.float32)
     for offset in range(KERNEL):

time: 711 us -> 750 us (1.055)
  waiting for transfers between devices: 496 us -> 536 us
    psum x1 -> x2, waiting for transfers between devices: 447 us -> 486 us  [part_page(): xin = lax.psum(xin, dev_i)]
  transfers between devices with their start and end apart: 10 -> 11, of which waited for: 6 -> 7; matrix products, arithmetic and copies ran while one was open for 18% -> 17% of each run, Pallas kernels for 0% -> 0%
where the time goes in v1:
time: 750 us; the launch traced here: 741 us
  waiting for transfers between devices  536 us (71%)
  other arithmetic  82 us (11%)
  local copies, waits for them, and re-layouts  40.2 us (5%)
  starting transfers between devices  36.2 us (5%)
  matrix products  31.2 us (4%)
  between operations  15.3 us (2%)
    psum x2, waiting for transfers between devices, part_page(): xin = lax.psum(xin, dev_i)  486 us
    unnamed x4, other arithmetic  43.7 us
    all_to_all x1, waiting for transfers between devices, local(): lax.all_to_all(context_heads[None], 'seq', split_axis=1, concat_axis=2, t...  35 us
    unnamed x25, local copies, waits for them, and re-layouts  22.1 us
  transfers between devices with their start and end apart: 11, of which 7 were waited for; matrix products, arithmetic and copies ran while one was open for 17% of the time, Pallas kernels for 0%

profile of v1, /device:TPU:1, one launch (start us, length us, event | category | flops | bytes accessed | tf_op | source)
XLA Modules:
  0.0 741.2 jit_solution(10455947053107178280)
XLA Ops:
  7.2 3.5 copy.31
  11.2 8.8 %reduce.66 = bf16[1536,192]{1,0:T(8,128)(2,1)S(1)} reduce(bf16[1536,1,192]{2,1,0:T(2,128)(2,1)S(1)} %bitcast.821, bf16[]{:T(256)} %broadcast.335), dimensions={1}, to_apply=%bitcast.766.reduce_sub_computation | reduce | bytes 1179650
  20.0 1.7 reshape.719
  21.8 9.2 %all-to-all-start = ((bf16[16,2,9216]{2,1,0:T(2,128)(2,1)}), bf16[16,2,9216]{2,1,0:T(2,128)(2,1)S(1)}, u32[]{:S(2)}, u32[]{:S(2)}) async-start(bf16[16,2,9216]{2,1,0:T(2,128)(2,1)} %reshape.719), calls=%async_computation | async-start | bytes 1179648 | tf_op jit(solution)/shard_map/all_to_all | solution.py:62
  32.2 8.8 %reduce.67 = bf16[1536,192]{1,0:T(8,128)(2,1)S(1)} reduce(bf16[1536,1,192]{2,1,0:T(2,128)(2,1)S(1)} %bitcast.823, bf16[]{:T(256)} %broadcast.335), dimensions={1}, to_apply=%bitcast.768.reduce_sub_computation | reduce | bytes 1179650
  41.0 1.7 reshape.721
  42.7 2.8 all-to-all-done
  45.5 5.7 all-to-all-start.1
  52.5 8.8 %reduce.68 = bf16[1536,192]{1,0:T(8,128)(2,1)S(1)} reduce(bf16[1536,1,192]{2,1,0:T(2,128)(2,1)S(1)} %bitcast.824, bf16[]{:T(256)} %broadcast.335), dimensions={1}, to_apply=%bitcast.770.reduce_sub_computation | reduce | bytes 1179650
  61.3 1.7 reshape.723
  63.0 2.2 all-to-all-done.1
  65.2 6.1 all-to-all-start.2
  78.0 1.3 copy.36
  80.2 5.1 all-to-all-done.2
  85.3 4.8 reshape.724
  91.8 1.3 copy.39
  94.0 28.7 %while.11 = (s32[]{:T(128)}, bf16[3,1024,1,96]{1,3,2,0:T(8,128)(2,1)S(1)}, bf16[3,1024,1,96]{1,3,2,0:T(8,128)(2,1)S(1)}, bf16[3072,1,96]{0,2,1:T(8,128)(2,1)S(1)...) while((s32[]{:T(128)}, bf16[3,1024,1,96]{1,3,2,0:T(8,128)(2,1)S(1)}, ...), condition=%wide.region_3.4_spmd.clone, body=%wide.region_0.3_spmd.clone.sunk | while | flops 1245807616 | bytes 39354456 | solution.py:50
  94.8 2.1 fusion.344
  96.9 2.7 fusion.345
  99.6 4.0 fusion.346
  104.3 2.1 fusion.344
  106.4 2.7 fusion.345
  109.1 4.0 fusion.346
  113.8 2.1 fusion.344
  115.9 2.7 fusion.345
  118.6 4.0 fusion.346
  123.4 17.2 %reduce.69 = bf16[3072,96]{1,0:T(8,128)(2,1)S(1)} reduce(bf16[3072,1,96]{2,1,0:T(2,128)(2,1)S(1)} %bitcast.822, bf16[]{:T(256)} %broadcast.335), dimensions={1}, to_apply=%bitcast.772.reduce_sub_computation | reduce | bytes 1179650
  140.6 2.0 reshape.725
  142.7 6.0 all-to-all-start.3
  149.7 35.0 %all-to-all-done.3 = bf16[16,2,9216]{2,1,0:T(2,128)(2,1)S(1)} async-done(((bf16[16,2,9216]{2,1,0:T(2,128)(2,1)}), bf16[16,2,9216]{2,1,0:T(2,128)(2,1)S(1)}, u32[]{:S(2)}, u32[]{:S(2)}) %all-to-all-start.3) | async-done | bytes 589856 | tf_op jit(solution)/shard_map/all_to_all | solution.py:73
  185.8 1.6 copy.43
  190.5 4.0 fusion.16
  194.7 2.4 collective-permute-start
  197.0 1.3 collective-permute-start.1
  198.5 3.9 collective-permute-done.1
  202.4 6.0 fusion.208
  208.4 1.3 collective-permute-start.2
  209.7 4.0 collective-permute-start.3
  213.7 7.6 %fusion.239 = (f32[1536]{0:T(1024)S(1)}, f32[1536]{0:T(1024)S(1)}, f32[1536]{0:T(1024)S(1)}, f32[1536]{0:T(1024)S(1)}, f32[1536]{0:T(1024)S(1)}, /*index=5*/f32[...) fusion(bf16[1,15,1536]{2,1,0:T(8,128)(2,1)S(1)} %collective-permute-done.1, ...), kind=kLoop, calls=%fused_computation.457 | loop fusion | flops 67820544 | bytes 3858624 | tf_op jit(solution)/shard_map/reduce_sum | solution.py:93
  221.4 1.4 fusion.240
  225.1 1.3 fusion.238
  226.4 1.4 fusion.225
  228.2 2.8 stack.127
  231.0 6.5 fusion.209
  237.5 154.4 %all-reduce.3.cloned.1.call-done = f32[31,1536]{1,0:T(8,128)} async-done(((f32[31,1536]{1,0:T(8,128)}), f32[31,1536]{1,0:T(8,128)}) %all-reduce.3.cloned.1.call-update) | async-done | bytes 190480 | tf_op jit(solution)/shard_map/psum | solution.py:13
  391.9 8.9 %fusion.17 = bf16[1,192,1536]{2,1,0:T(8,128)(2,1)} fusion(bf16[1536,1536]{0,1:T(8,128)(2,1)} %all-gather.2.cloned.1.call-done, bf16[1,192,1536]{2,1,0:T(8,128)(2,1)S(1)} %copy-done, bf16[1,192,1536]{2,1,0:T(8,128)(2,1)S(1)} %fusion.208, bf16[1,15,1536]{2,1,0:T(8,128)(2,1)S(1)} %collective-permute-done.3, ...), kind=kOutput, calls=%fused_computation.109 | convolution fusion | flops 961118208 | bytes 6770880 | tf_op jit(solution)/shard_map/dot_general | solution.py:107
  400.9 332.0 %all-reduce.5.cloned.1.call-done = f32[31,1536]{1,0:T(8,128)} async-done(((f32[31,1536]{1,0:T(8,128)}), f32[31,1536]{1,0:T(8,128)}) %all-reduce.5.cloned.1.call-update) | async-done | bytes 190480 | tf_op jit(solution)/shard_map/psum | solution.py:13
  732.9 1.6 broadcast_multiply_fusion
  (86 shorter events, 22.9 us)
Async XLA Ops:
  20.0 10.9 %copy-start.1 = (bf16[1,192,1536]{2,1,0:T(8,128)(2,1)S(1)}, bf16[1,192,1536]{2,1,0:T(8,128)(2,1)}, u32[]{:S(2)}) copy-start(bf16[1,192,1536]{2,1,0:T(8,128)(2,1)} %param.12) | copy-start | bytes 1769476
  21.8 23.8 %all-to-all-start = ((bf16[16,2,9216]{2,1,0:T(2,128)(2,1)}), bf16[16,2,9216]{2,1,0:T(2,128)(2,1)S(1)}, u32[]{:S(2)}, u32[]{:S(2)}) async-start(bf16[16,2,9216]{2,1,0:T(2,128)(2,1)} %reshape.719), calls=%async_computation | async-start | bytes 1179648 | tf_op jit(solution)/shard_map/all_to_all | solution.py:62
  42.7 8.5 %copy-start.2 = (bf16[1,192,1536]{2,1,0:T(8,128)(2,1)S(1)}, bf16[1,192,1536]{2,1,0:T(8,128)(2,1)}, u32[]{:S(2)}) copy-start(bf16[1,192,1536]{2,1,0:T(8,128)(2,1)} %param.13) | copy-start | bytes 1769476
  45.5 19.7 %all-to-all-start.1 = ((bf16[16,2,9216]{2,1,0:T(2,128)(2,1)}), bf16[16,2,9216]{2,1,0:T(2,128)(2,1)S(1)}, u32[]{:S(2)}, u32[]{:S(2)}) async-start(bf16[16,2,9216]{2,1,0:T(2,128)(2,1)} %reshape.721), calls=%async_computation.1 | async-start | bytes 1179648 | tf_op jit(solution)/shard_map/all_to_all | solution.py:63
  65.2 20.1 %all-to-all-start.2 = ((bf16[16,2,9216]{2,1,0:T(2,128)(2,1)}), bf16[16,2,9216]{2,1,0:T(2,128)(2,1)}, u32[]{:S(2)}, u32[]{:S(2)}) async-start(bf16[16,2,9216]{2,1,0:T(2,128)(2,1)} %reshape.723), calls=%async_computation.2 | async-start | bytes 1179648 | tf_op jit(solution)/shard_map/all_to_all | solution.py:64
  71.4 119.1 %all-gather.2.cloned.1.call-start = ((), (), s32[]{:S(2)}) async-start(), calls=%async_computation.4 | async-start | bytes 4866048 | tf_op jit(solution)/shard_map/all_gather | solution.py:76
  91.8 2.2 copy-start.3
  140.6 8.8 %copy-start.4 = (f32[31,1536]{1,0:T(8,128)S(1)}, f32[31,1536]{1,0:T(8,128)}, u32[]{:S(2)}) copy-start(f32[31,1536]{1,0:T(8,128)} %param.16) | copy-start | bytes 571396
  142.7 42.0 %all-to-all-start.3 = ((bf16[16,2,9216]{2,1,0:T(2,128)(2,1)}), bf16[16,2,9216]{2,1,0:T(2,128)(2,1)S(1)}, u32[]{:S(2)}, u32[]{:S(2)}) async-start(bf16[16,2,9216]{2,1,0:T(2,128)(2,1)} %reshape.725), calls=%async_computation.3 | async-start | bytes 1179648 | tf_op jit(solution)/shard_map/all_to_all | solution.py:73
  148.7 243.2 %all-reduce.3.cloned.1.call-start = ((), (), s32[]{:S(2)}) async-start(), calls=%async_computation.5 | async-start | bytes 393216 | tf_op jit(solution)/shard_map/psum | solution.py:13
  188.3 2.2 copy-start.5
  194.5 7.9 %copy-start = (bf16[1,192,1536]{2,1,0:T(8,128)(2,1)S(1)}, bf16[1,192,1536]{2,1,0:T(8,128)(2,1)}, u32[]{:S(2)}) copy-start(bf16[1,192,1536]{2,1,0:T(8,128)(2,1)} %param.17) | copy-start | bytes 1769476
  194.7 3.9 collective-permute-start
  197.0 5.4 collective-permute-start.1
  208.4 22.6 %collective-permute-start.2 = (bf16[1,15,1536]{2,1,0:T(8,128)(2,1)S(1)}, bf16[1,15,1536]{2,1,0:T(8,128)(2,1)S(1)}, u32[]{:S(2)}, u32[]{:S(2)}) collective-permute-start(bf16[1,15,1536]{2,1,0:T(8,128)(2,1)S(1)} %get-tuple-element.152), channel_id=1, source_target_pairs={{32,0},{64,32},{96,64},{128,96},{160,128},{192,160},{224,192},{256... | collective-permute-start | bytes 138248 | tf_op jit(solution)/shard_map/ppermute | solution.py:25
  209.7 21.3 %collective-permute-start.3 = (bf16[1,15,1536]{2,1,0:T(8,128)(2,1)S(1)}, bf16[1,15,1536]{2,1,0:T(8,128)(2,1)S(1)}, u32[]{:S(2)}, u32[]{:S(2)}) collective-permute-start(bf16[1,15,1536]{2,1,0:T(8,128)(2,1)S(1)} %get-tuple-element.153), channel_id=1, source_target_pairs={{0,32},{32,64},{64,96},{96,128},{128,160},{160,192},{192,224},{224... | collective-permute-start | bytes 138248 | tf_op jit(solution)/shard_map/ppermute | solution.py:22
  231.0 501.9 %all-reduce.5.cloned.1.call-start = ((), (), s32[]{:S(2)}) async-start(), calls=%async_computation.6 | async-start | bytes 393216 | tf_op jit(solution)/shard_map/psum | solution.py:13
Sparse Core Ops, SparseCore 0:
  75.3 107.3 all-gather.1
  231.1 160.7 all-reduce.2
  395.1 337.7 all-reduce.4
